TPU v7x, 256 devices: a whole 4x4x8 slice. The times are simulated.
256 devices in a mesh: scene: 8 (over z_lo, core), row: 8 (over x, z_hi), col: 4 (over y).
Axes of the slice: x: 4, y: 4, z: 8 (z_hi: 2, z_lo: 4; z = z_hi * 4 + z_lo), core: 2. Of those that a mesh axis runs over, the one named last changes fastest.
Arguments:
- scene: bfloat16 [1024, 256, 768], P(('scene', 'row'), 'col'), parts along dimension 0, may hold values from -6 to 6
- cotangent: bfloat16 [1024, 256, 768], P(('scene', 'row'), 'col'), parts along dimension 0, may hold values from -6 to 6
- query_key_value_weight: bfloat16 [768, 2304], replicated
- proj_weight: bfloat16 [768, 768], replicated, may hold values from -0.21875 to 0.21875
- kept: int32 [256, 16], P('scene'), parts along dimension 0, may hold values from 0 to 1, as said below
Outputs:
- scene_grad: bfloat16 [1024, 256, 768], P(('scene', 'row'), 'col'), parts along dimension 0
- qkv_grad: float32 [6144, 2304], P(('scene', 'row', 'col')), parts along dimension 0
- proj_grad: float32 [6144, 768], P(('scene', 'row', 'col')), parts along dimension 0
There are 8 independent parts, one for each index of `scene`. A program takes and returns all parts, laid end to end along the dimension named above; an argument that names none is the same for every part. Nothing has to cross between parts.
Inputs may be any that keep to these rules, and one draw needn't show every extreme that they name: Within each column of tiles (same second device-grid index) exactly 48 windows are kept; no tile keeps more than 12 windows and in every column of tiles some tile keeps exactly 12.
All inputs are finite; a program needn't handle non-finite values.
Results may differ from a plain program's by a relative error of at most 0.0085.
Values may be sent and summed in bfloat16 or wider, within the bound.
A program may use at most 128 MiB of HBM per device.

v0:
```python
import jax
import jax.numpy as jnp
from jax import lax
from jax.sharding import PartitionSpec as P

HD = 32
WIN = 8
KEEP_DEV = 6


def shifted(block, axis, distance):
    devices = range(lax.axis_size(axis))
    route = [((i - distance) % len(devices), i) for i in devices]
    return lax.ppermute(block, axis, route)


def window_bias(grow, gcol, height, span):
    offs = jnp.arange(WIN, dtype=jnp.int32)
    rows = grow[:, None] * WIN + offs[None, :]
    cols = gcol[:, None] * WIN + offs[None, :]
    row_label = (rows >= height - WIN).astype(jnp.int32) + (rows >= height - WIN // 2).astype(
        jnp.int32
    )
    col_label = (cols >= span - WIN).astype(jnp.int32) + (cols >= span - WIN // 2).astype(jnp.int32)
    label = (3 * row_label[:, :, None] + col_label[:, None, :]).reshape(grow.shape[0], WIN * WIN)
    same = label[:, :, None] == label[:, None, :]
    return jnp.where(same, 0.0, -100.0).astype(jnp.float32)


def window_grads(xw, gw, query_key_value_weight, proj_weight, bias):
    count, area, width = xw.shape
    heads = width // HD
    single_precision = jnp.float32
    xf = xw.astype(single_precision)
    input_mean = jnp.mean(xf, axis=-1, keepdims=True)
    centered_input = xf - input_mean
    inverse_deviation = lax.rsqrt(
        jnp.mean(centered_input * centered_input, axis=-1, keepdims=True) + 1e-05
    )
    normed_input = centered_input * inverse_deviation
    input_block = normed_input.astype(jnp.bfloat16)
    qkv = jnp.einsum(
        "nsd,de->nse", input_block, query_key_value_weight, preferred_element_type=single_precision
    ).astype(jnp.bfloat16)
    query = qkv[:, :, :width].reshape(count, area, heads, HD)
    keys = qkv[:, :, width : 2 * width].reshape(count, area, heads, HD)
    values = qkv[:, :, 2 * width :].reshape(count, area, heads, HD)
    scale = HD ** (-0.5)
    scores = (
        jnp.einsum("nqhc,nkhc->nhqk", query, keys, preferred_element_type=single_precision) * scale
        + bias[:, None]
    )
    top = jnp.max(scores, axis=-1, keepdims=True)
    expo = jnp.exp(scores - top)
    probs = expo / jnp.sum(expo, axis=-1, keepdims=True)
    pb = probs.astype(jnp.bfloat16)
    attended = (
        jnp.einsum("nhqk,nkhc->nqhc", pb, values, preferred_element_type=single_precision)
        .reshape(count, area, width)
        .astype(jnp.bfloat16)
    )
    d_att = jnp.einsum(
        "jkp,wp->jkw", gw, proj_weight, preferred_element_type=single_precision
    ).astype(jnp.bfloat16)
    proj_part = jnp.einsum("nsd,nse->de", attended, gw, preferred_element_type=single_precision)
    d_heads = d_att.reshape(count, area, heads, HD)
    d_p = jnp.einsum("nqhc,nkhc->nhqk", d_heads, values, preferred_element_type=single_precision)
    d_v = jnp.einsum(
        "nhqk,nqhc->nkhc", pb, d_heads, preferred_element_type=single_precision
    ).astype(jnp.bfloat16)
    d_s = (probs * (d_p - jnp.sum(probs * d_p, axis=-1, keepdims=True)) * scale).astype(
        jnp.bfloat16
    )
    d_q = jnp.einsum("nhqk,nkhc->nqhc", d_s, keys, preferred_element_type=single_precision).astype(
        jnp.bfloat16
    )
    d_k = jnp.einsum("nhqk,nqhc->nkhc", d_s, query, preferred_element_type=single_precision).astype(
        jnp.bfloat16
    )
    projected_gradient = jnp.concatenate(
        [
            d_q.reshape(count, area, width),
            d_k.reshape(count, area, width),
            d_v.reshape(count, area, width),
        ],
        axis=-1,
    )
    qkv_part = jnp.einsum(
        "nsd,nse->de", input_block, projected_gradient, preferred_element_type=single_precision
    )
    normed_gradient = jnp.einsum(
        "jkp,wp->jkw",
        projected_gradient,
        query_key_value_weight,
        preferred_element_type=single_precision,
    )
    branch_index = inverse_deviation * (
        normed_gradient
        - jnp.mean(normed_gradient, axis=-1, keepdims=True)
        - normed_input * jnp.mean(normed_gradient * normed_input, axis=-1, keepdims=True)
    )
    return (branch_index.astype(jnp.bfloat16), qkv_part, proj_part)


def on_device(scene, cotangent, query_key_value_weight, proj_weight, kept):
    tile_rows, tile_cols, width = scene.shape
    half = WIN // 2
    nrow = lax.axis_size("row")
    ncol = lax.axis_size("col")
    row_index = lax.axis_index("row")
    col_index = lax.axis_index("col")
    height = tile_rows * nrow
    span = tile_cols * ncol
    wrows = tile_rows // WIN
    wcols = tile_cols // WIN
    wtile = wrows * wcols
    area = WIN * WIN
    most = 2 * KEEP_DEV
    paired = jnp.stack([scene, cotangent])
    ahead = shifted(paired[:, :half], "row", -1)
    paired = jnp.concatenate([paired[:, half:], ahead], axis=1)
    ahead = shifted(paired[:, :, :half], "col", -1)
    paired = jnp.concatenate([paired[:, :, half:], ahead], axis=2)
    windows = (
        paired.reshape(2, wrows, WIN, wcols, WIN, width)
        .transpose(0, 1, 3, 2, 4, 5)
        .reshape(2, wtile, area, width)
    )
    counts = jnp.sum(kept, axis=1)
    order = jnp.argsort(1 - kept, axis=1, stable=True)
    myself = row_index * ncol + col_index
    my_order = lax.dynamic_index_in_dim(order, myself, 0, keepdims=False)
    local = my_order[:most]
    mine = lax.dynamic_index_in_dim(counts, myself, 0, keepdims=False)
    valid = (jnp.arange(most, dtype=jnp.int32) < mine).astype(jnp.bfloat16)
    xw = windows[0][local]
    gw = windows[1][local] * valid[:, None, None]
    grow = myself // ncol * wrows + local // wcols
    gcol = myself % ncol * wcols + local % wcols
    grow, gcol = (grow, gcol)
    dxw, qkv_part, proj_part = window_grads(
        xw, gw, query_key_value_weight, proj_weight, window_bias(grow, gcol, height, span)
    )
    branch_index = jnp.zeros((wtile, area, width), jnp.bfloat16).at[local].set(dxw)
    branch_index = (
        branch_index.reshape(wrows, wcols, WIN, WIN, width)
        .transpose(0, 2, 1, 3, 4)
        .reshape(tile_rows, tile_cols, width)
    )
    behind = shifted(branch_index[:, tile_cols - half :], "col", 1)
    branch_index = jnp.concatenate([behind, branch_index[:, : tile_cols - half]], axis=1)
    behind = shifted(branch_index[tile_rows - half :], "row", 1)
    branch_index = jnp.concatenate([behind, branch_index[: tile_rows - half]], axis=0)
    scene_grad = (cotangent.astype(jnp.float32) + branch_index.astype(jnp.float32)).astype(
        jnp.bfloat16
    )
    qkv_grad, proj_grad = (
        lax.psum_scatter(qkv_part, ("row", "col"), scatter_dimension=0, tiled=True),
        lax.psum_scatter(proj_part, ("row", "col"), scatter_dimension=0, tiled=True),
    )
    return (scene_grad, qkv_grad, proj_grad)


def solution(mesh):
    return jax.shard_map(
        on_device,
        mesh=mesh,
        in_specs=(
            P(("scene", "row"), "col", None),
            P(("scene", "row"), "col", None),
            P(),
            P(),
            P("scene", None),
        ),
        out_specs=(
            P(("scene", "row"), "col", None),
            P(("scene", "row", "col"), None),
            P(("scene", "row", "col"), None),
        ),
        check_vma=False,
    )
```

profile of v0, /device:TPU:32, one launch (start us, length us, event | category | flops | bytes accessed | tf_op | source)
XLA Modules:
  0.0 661.3 jit_solution(2891516454004423957)
XLA Ops:
  7.2 2.2 pad_maximum_fusion.5
  9.5 8.5 %collective-permute-start = (bf16[2,4,64,768]{3,2,1,0:T(8,128)(2,1)}, bf16[2,4,64,768]{3,2,1,0:T(8,128)(2,1)}, u32[]{:S(2)}, u32[]{:S(2)}) collective-permute-start(bf16[2,4,64,768]{3,2,1,0:T(8,128)(2,1)} %pad_maximum_fusion.5), channel_id=1, source_target_pairs={{4,0},{8,4},{12,8},{16,12},{20,16},{24,20},{28,24},{0,28},{5,1},{9... | collective-permute-start | bytes 2359304 | tf_op jit(solution)/shard_map/ppermute | solution.py:14
  21.5 1.3 dynamic_slice.9
  23.5 1.1 compare_convert_fusion
  26.1 1.8 fusion.27
  27.9 0.9 compare_select_fusion
  28.9 23.1 %collective-permute-done = bf16[2,4,64,768]{3,2,1,0:T(8,128)(2,1)} collective-permute-done((bf16[2,4,64,768]{3,2,1,0:T(8,128)(2,1)}, bf16[2,4,64,768]{3,2,1,0:T(8,128)(2,1)}, u32[]{:S(2)}, u32[]{:S(2)}) %collective-permute-start) | collective-permute-done | bytes 786464 | tf_op jit(solution)/shard_map/ppermute | solution.py:14
  51.9 1.0 pad_maximum_fusion.7
  52.9 3.3 collective-permute-start.1
  56.1 1.9 slice_maximum_fusion
  58.0 1.3 collective-permute-done.1
  59.8 1.4 fusion.70
  61.2 1.3 copy.51
  62.5 3.1 gather_fusion
  65.6 1.6 convert_reduce_fusion
  67.2 1.7 fusion.26
  69.0 3.3 convolution_convert_fusion
  72.2 1.9 fusion.69
  74.1 3.7 copy.52
  77.8 3.7 copy.53
  81.5 3.7 copy.57
  85.3 2.7 copy.55
  88.0 3.2 gather_fusion.1
  91.2 10.5 %fusion.72 = (f32[12,24,64]{2,1,0:T(8,128)}, f32[12,24,64,64]{2,3,1,0:T(8,128)}) fusion(f32[12,64,64]{1,2,0:T(8,128)} %compare_select_fusion, bf16[12,64,24,32]{1,3,2,0:T(8,128)(2,1)} %bitcast.73, bf16[12,64,24,32]{1,3,2,0:T(8,128)(2,1)} %bitcast.75), kind=kOutput, calls=%fused_computation.100 | convolution fusion | flops 80216128 | bytes 7348224 | tf_op jit(solution)/shard_map/sub | solution.py:54
  101.7 5.8 fusion.35
  107.5 2.7 convolution_bitcast_fusion.1
  110.5 3.8 convolution_convert_fusion.1
  114.3 3.7 copy.56
  118.0 7.5 %fusion.73 = f32[12,24,64,64]{2,3,1,0:T(8,128)} fusion(bf16[12,64,24,32]{1,3,2,0:T(8,128)(2,1)} %bitcast.67, bf16[12,64,24,32]{1,3,2,0:T(8,128)(2,1)} %bitcast.66), kind=kOutput, calls=%fused_computation.101 | convolution fusion | flops 75497472 | bytes 7077888 | tf_op jit(solution)/shard_map/nqhc,nkhc->nhqk/dot_general | solution.py:67
  125.5 16.9 %fusion.38 = bf16[12,24,32,64]{3,2,1,0:T(8,128)(2,1)} fusion(bf16[12,64,24,32]{1,3,2,0:T(8,128)(2,1)} %bitcast.76, f32[12,24,64,64]{2,3,1,0:T(8,128)} %fusion.73, f32[12,24,64,64]{2,3,1,0:T(8,128)} %get-tuple-element.17, f32[12,24,64]{2,1,0:T(8,128)} %get-tuple-element.16), kind=kOutput, calls=%fused_computation.46 | convolution fusion | flops 84363328 | bytes 11870208 | tf_op jit(solution)/shard_map/nhqk,nkhc->nqhc/dot_general | solution.py:74
  142.4 3.8 copy.61
  146.2 17.2 %fusion.41 = bf16[12,24,32,64]{3,2,1,0:T(8,128)(2,1)} fusion(bf16[12,64,24,32]{1,3,2,0:T(8,128)(2,1)} %bitcast.74, f32[12,24,64,64]{2,3,1,0:T(8,128)} %fusion.73, f32[12,24,64,64]{2,3,1,0:T(8,128)} %get-tuple-element.17, f32[12,24,64]{2,1,0:T(8,128)} %get-tuple-element.16), kind=kOutput, calls=%fused_computation.47 | convolution fusion | flops 84363328 | bytes 11870208 | tf_op jit(solution)/shard_map/nhqk,nqhc->nkhc/dot_general | solution.py:77
  163.4 3.8 copy.62
  167.2 8.4 %fusion.32 = bf16[12,24,32,64]{3,2,1,0:T(8,128)(2,1)} fusion(bf16[12,64,24,32]{1,3,2,0:T(8,128)(2,1)} %bitcast.68, f32[12,24,64,64]{2,3,1,0:T(8,128)} %get-tuple-element.17, f32[12,24,64]{2,1,0:T(8,128)} %get-tuple-element.16), kind=kOutput, calls=%fused_computation.44 | convolution fusion | flops 78446592 | bytes 7151616 | tf_op jit(solution)/shard_map/nhqk,nqhc->nkhc/dot_general | solution.py:68
  175.6 3.8 copy.63
  179.5 8.4 %convolution_bitcast_fusion = f32[768,2304]{1,0:T(8,128)} fusion(bf16[12,64,768]{2,1,0:T(8,128)(2,1)} %copy.63, bf16[12,64,768]{2,1,0:T(8,128)(2,1)} %copy.62, bf16[12,64,768]{2,1,0:T(8,128)(2,1)} %copy.61, bf16[12,64,768]{2,1,0:T(8,128)(2,1)} %gather_fusion, f32[12,64]{1,0:T(8,128)S(1)} %add_rsqrt_fusion, f32[12,64]{1,0:T(8,128)S(1)} %broadcast_multiply_fusion.2), kind=kOutput, calls=%fused_computation.11 | convolution fusion | flops 2730885120 | bytes 11802624 | tf_op jit(solution)/shard_map/nsd,nse->de/dot_general | solution.py:88
  187.9 5.5 fusion.68
  193.4 1.7 fusion.25
  195.1 1.3 broadcast_in_dim.8
  196.4 5.3 scatter_fusion
  201.7 1.7 copy.64
  203.5 1.1 collective-permute-start.2
  204.6 5.3 collective-permute-done.2
  210.0 5.3 collective-permute-start.3
  215.2 18.2 %collective-permute-done.3 = bf16[4,64,768]{2,1,0:T(8,128)(2,1)S(1)} collective-permute-done((bf16[4,64,768]{2,1,0:T(8,128)(2,1)S(1)}, bf16[4,64,768]{2,1,0:T(8,128)(2,1)S(1)}, u32[]{:S(2)}, u32[]{:S(2)}) %collective-permute-start.3) | collective-permute-done | bytes 393248 | tf_op jit(solution)/shard_map/ppermute | solution.py:14
  233.4 1.8 add_convert_fusion
  235.3 142.0 %reduce-scatter.5.cloned.1.call-done = f32[24,768]{1,0:T(8,128)} async-done(((f32[768,768]{1,0:T(8,128)}), f32[24,768]{1,0:T(8,128)}) %reduce-scatter.5.cloned.1.call-update) | async-done | bytes 73744 | tf_op jit(solution)/shard_map/reduce_scatter | solution.py:159
  377.3 277.2 %reduce-scatter.3.cloned.1.call-done = f32[24,2304]{1,0:T(8,128)} async-done(((f32[768,2304]{1,0:T(8,128)}), f32[24,2304]{1,0:T(8,128)}) %reduce-scatter.3.cloned.1.call-update) | async-done | bytes 221200 | tf_op jit(solution)/shard_map/reduce_scatter | solution.py:158
  (40 shorter events, 6.7 us)
Async XLA Ops:
  7.2 61.8 %copy-start = (bf16[768,2304]{1,0:T(8,128)(2,1)S(1)}, bf16[768,2304]{1,0:T(8,128)(2,1)}, u32[]{:S(2)}) copy-start(bf16[768,2304]{1,0:T(8,128)(2,1)} %param.7) | copy-start | bytes 10616836
  7.2 10.8 %copy-start.5 = (s32[32,16]{0,1:T(8,128)S(1)}, s32[32,16]{0,1:T(8,128)}, u32[]{:S(2)}) copy-start(s32[32,16]{0,1:T(8,128)} %param.9) | copy-start | bytes 6148
  7.2 370.1 %reduce-scatter.5.cloned.1.call-start = ((), (), s32[]{:S(2)}) async-start(), calls=%async_computation.3 | async-start | bytes 2433024 | tf_op jit(solution)/shard_map/reduce_scatter | solution.py:159
  9.5 42.5 %collective-permute-start = (bf16[2,4,64,768]{3,2,1,0:T(8,128)(2,1)}, bf16[2,4,64,768]{3,2,1,0:T(8,128)(2,1)}, u32[]{:S(2)}, u32[]{:S(2)}) collective-permute-start(bf16[2,4,64,768]{3,2,1,0:T(8,128)(2,1)} %pad_maximum_fusion.5), channel_id=1, source_target_pairs={{4,0},{8,4},{12,8},{16,12},{20,16},{24,20},{28,24},{0,28},{5,1},{9... | collective-permute-start | bytes 2359304 | tf_op jit(solution)/shard_map/ppermute | solution.py:14
  25.5 0.6 copy-start.7
  26.1 36.5 %copy-start.6 = (s32[1024]{0:T(1024)}, s32[1024]{0:T(1024)S(1)}, u32[]{:S(2)}) copy-start(s32[1024]{0:T(1024)S(1)} %pad_clamp_fusion) | copy-start | bytes 12292
  52.9 6.5 collective-permute-start.1
  65.6 3.4 copy-start.1
  101.7 5.8 copy-start.4
  101.7 5.8 copy-start.8
  110.2 544.2 %reduce-scatter.3.cloned.1.call-start = ((), (), s32[]{:S(2)}) async-start(), calls=%async_computation.2 | async-start | bytes 7299072 | tf_op jit(solution)/shard_map/reduce_scatter | solution.py:158
  187.9 5.5 copy-start.2
  201.7 31.7 %copy-start.3 = (bf16[16,64,768]{2,1,0:T(8,128)(2,1)S(1)}, bf16[16,64,768]{2,1,0:T(8,128)(2,1)}, u32[]{:S(2)}) copy-start(bf16[16,64,768]{2,1,0:T(8,128)(2,1)} %param.6) | copy-start | bytes 4718596
  203.5 6.4 collective-permute-start.2
  210.0 23.4 %collective-permute-start.3 = (bf16[4,64,768]{2,1,0:T(8,128)(2,1)S(1)}, bf16[4,64,768]{2,1,0:T(8,128)(2,1)S(1)}, u32[]{:S(2)}, u32[]{:S(2)}) collective-permute-start(bf16[4,64,768]{2,1,0:T(8,128)(2,1)S(1)} %pad_maximum_fusion.6), channel_id=1, source_target_pairs={{28,0},{0,4},{4,8},{8,12},{12,16},{16,20},{20,24},{24,28},{29,1},{... | collective-permute-start | bytes 1179656 | tf_op jit(solution)/shard_map/ppermute | solution.py:14
Sparse Core Ops, SparseCore 0:
  110.4 266.8 reduce-scatter.4
  383.5 270.8 reduce-scatter.2
where the time goes:
time: 663 us; the launch traced here: 661 us
  waiting for transfers between devices  467 us (70%)
  matrix products  89.9 us (14%)
  local copies, waits for them, and re-layouts  52 us (8%)
  other arithmetic  19.7 us (3%)
  starting transfers between devices  18.4 us (3%)
  between operations  14.2 us (2%)
    reduce_scatter x1, waiting for transfers between devices, on_device(): lax.psum_scatter(qkv_part, ('row', 'col'), scatter_dimension=0, tiled=True)  277 us
    reduce_scatter x1, waiting for transfers between devices, on_device(): lax.psum_scatter(proj_part, ('row', 'col'), scatter_dimension=0, tiled=True)  142 us
    ppermute x4, waiting for transfers between devices, shifted(): return lax.ppermute(block, axis, route)  47.9 us
    ppermute x4, starting transfers between devices, shifted(): return lax.ppermute(block, axis, route)  18.1 us
    dot_general x1, matrix products, window_grads(): jnp.einsum('nhqk,nqhc->nkhc', d_s, query, preferred_element_type=single_p...  17.2 us
    dot_general x1, matrix products, window_grads(): jnp.einsum('nhqk,nkhc->nqhc', d_s, keys, preferred_element_type=single_pr...  16.9 us
  transfers between devices with their start and end apart: 6, of which 6 were waited for; matrix products, arithmetic and copies ran while one was open for 16% of the time, Pallas kernels for 0%

commit v1 on v0

v1 whole, which is shorter than its diff:
```python
import functools

import jax
import jax.numpy as jnp
from jax import lax
from jax.experimental import pallas as pl
from jax.experimental.pallas import tpu as pltpu
from jax.sharding import PartitionSpec as P

HD = 32
WIN = 8
HALF = 4
AREA = 64
PACK = 4
GROUP = PACK * HD
BATCH = 4 * AREA
F32 = jnp.float32
BF16 = jnp.bfloat16
NT = (((1,), (1,)), ((), ()))
TN = (((0,), (0,)), ((), ()))


def dot(a, b, dims=(((1,), (0,)), ((), ()))):
    return lax.dot_general(a, b, dims, preferred_element_type=F32)


def swap_halves(tile):
    return pltpu.roll(tile, HALF, tile.ndim - 2)


def kernel(names, *refs):
    r = dict(zip(names, refs))
    scene, cot = r["scene"], r["cotangent"]
    xg, br, stash_d, stash_g = r["xg"], r["br"], r["stash_d"], r["stash_g"]
    stash_xt, stash_at = r["stash_xt"], r["stash_at"]
    xb_s, xh_s, inv_s, qkv_s, dat_s, att_s = (
        r["xb"], r["xh"], r["inv"], r["qkv"], r["dat"], r["att"],
    )
    wqkv, wp = r["wqkv"], r["wp"]
    tile_rows, tile_cols, width = scene.shape
    groups = width // GROUP
    row, col = lax.axis_index("row"), lax.axis_index("col")
    nrow, ncol = lax.axis_size("row"), lax.axis_size("col")
    x_at, z_at = row // 2, row % 2
    myself = row * ncol + col

    def at(drow, dcol):
        return {"row": (row + drow + nrow) % nrow, "col": (col + dcol + ncol) % ncol}

    def send(number, src, dst, device):
        return pltpu.make_async_remote_copy(
            src_ref=src,
            dst_ref=dst,
            send_sem=r["send_sems"].at[number],
            recv_sem=r["recv_sems"].at[number],
            device_id=device,
            device_id_type=pl.DeviceIdType.MESH,
        )

    own = pl.ds(0, tile_rows)
    loads = [
        pltpu.make_async_copy(src, dst, r["load_sems"].at[k])
        for k, (src, dst) in enumerate(
            [
                (scene, xg.at[0, own, pl.ds(0, tile_cols)]),
                (cot, xg.at[1, own, pl.ds(0, tile_cols)]),
                (r["wqkv_hbm"], wqkv),
                (r["wp_hbm"], wp),
            ]
        )
    ]
    for load in loads:
        load.start()

    z_across = 1 - 2 * z_at
    partners = [(-1, 0), (1, 0), (0, -1), (0, 1), (-1, -1), (1, 1), (2, 0), (-2, 0)]
    barrier = pltpu.get_barrier_semaphore()
    for partner in partners:
        pl.semaphore_signal(
            barrier, inc=1, device_id=at(*partner), device_id_type=pl.DeviceIdType.MESH
        )
    pl.semaphore_wait(barrier, len(partners))

    def row_halo(array, half):
        src = (scene, cot)[array]
        columns = pl.ds(half * 2 * 16, 2 * 16)
        return send(
            2 * half + array,
            src.at[pl.ds(0, HALF), columns],
            xg.at[array, pl.ds(tile_rows, HALF), columns],
            at(-1, 0),
        )

    for half in (1, 0):
        for array in (0, 1):
            row_halo(array, half).start()

    low = lax.broadcasted_iota(jnp.int32, (WIN, width), 0) < HALF

    loads[0].wait()
    loads[1].wait()

    def pack_columns(k, _):
        for array in (0, 1):
            pair = xg[array, pl.ds(2 * k, 2), pl.ds(0, 16)].astype(F32)[:, :WIN]
            tile = jnp.where(low, pair[0], swap_halves(pair[1]))
            r["edge_f"][array, pl.ds(pl.multiple_of(k * WIN, WIN), WIN)] = tile
        return 0

    lax.fori_loop(0, tile_rows // 2, pack_columns, 0)
    r["edge_out"][...] = r["edge_f"][...].astype(BF16)

    edge_in = r["edge_in"]
    tokens = tile_rows * HALF
    col_halo = send(
        4,
        r["edge_out"].at[:, pl.ds(16, tokens - 16)],
        edge_in.at[:, pl.ds(0, tokens - 16)],
        at(0, -1),
    )
    corner = send(
        5, r["edge_out"].at[:, pl.ds(0, 16)], edge_in.at[:, pl.ds(tokens - 16, 16)], at(-1, -1)
    )
    col_halo.start()
    corner.start()

    def unpack_columns(first, count):
        def body(k, _):
            for array in (0, 1):
                both = edge_in[array, pl.ds(pl.multiple_of(k * 16, 16), 16)].astype(F32)
                for n in (0, 1):
                    tile = both[n * WIN : (n + 1) * WIN]
                    for odd in (0, 1):
                        part = swap_halves(tile) if odd else tile
                        whole = jnp.concatenate([part, jnp.zeros_like(part)], axis=0)
                        xg[array, HALF + 4 * k + 2 * n + odd, pl.ds(tile_cols, 16)] = whole.astype(
                            BF16
                        )
            return 0

        lax.fori_loop(first, first + count, body, 0)

    for load in loads[2:]:
        load.wait()

    edge_ret, left_in = r["edge_ret"], r["left_in"]
    col_back = send(
        6, edge_ret.at[pl.ds(0, tokens - 16)], left_in.at[pl.ds(16, tokens - 16)], at(0, 1)
    )
    corner_back = send(
        7, edge_ret.at[pl.ds(tokens - 16, 16)], left_in.at[pl.ds(0, 16)], at(1, 1)
    )

    def row_back(half):
        columns = pl.ds(half * 2 * 16, 2 * 16)
        return send(
            8 + half,
            br.at[pl.ds(tile_rows, HALF), columns],
            br.at[pl.ds(0, HALF), columns],
            at(1, 0),
        )

    scale = HD ** (-0.5)
    lane_head = lax.broadcasted_iota(jnp.int32, (AREA, GROUP), 1) // HD
    key_at = lax.broadcasted_iota(jnp.int32, (AREA, PACK * AREA), 0)
    query_at = lax.broadcasted_iota(jnp.int32, (AREA, PACK * AREA), 1) % AREA
    row_differs = jnp.where(key_at // 32 != query_at // 32, 1, 0)
    col_differs = jnp.where((key_at % 8) // 4 != (query_at % 8) // 4, 1, 0)

    def spread(block):
        zero = jnp.zeros_like(block)
        return jnp.concatenate([jnp.where(lane_head == h, block, zero) for h in range(PACK)], axis=0)

    def gather_heads(full):
        total = full[:AREA]
        for h in range(1, PACK):
            total = jnp.where(lane_head == h, full[h * AREA : (h + 1) * AREA], total)
        return total

    def batch(b, _):
        i = b // 2
        half = (b % 2 + b // 2) % 2

        @pl.when(b == 1)
        def _():
            col_halo.wait_recv()
            unpack_columns(0, (tile_rows - HALF) // 4)

        @pl.when(b == 2)
        def _():
            row_halo(0, 1).wait_recv()
            row_halo(1, 1).wait_recv()
            corner.wait_recv()
            unpack_columns((tile_rows - HALF) // 4, 1)

        @pl.when(b == 3)
        def _():
            row_halo(0, 0).wait_recv()
            row_halo(1, 0).wait_recv()

        first = pl.multiple_of(b * BATCH, BATCH)

        def normalise(n, _):
            pair, rows = n // 4, n % 4
            m = 2 * half + pair
            top = WIN * i + HALF + 2 * rows
            here = pl.ds(pl.multiple_of(16 * m, 16), 16)
            following = pl.ds(pl.multiple_of(16 * m + 16, 16), 16)
            for array in (0, 1):
                t0 = xg[array, pl.ds(top, 2), here].astype(F32)
                t1 = xg[array, pl.ds(top, 2), following].astype(F32)
                lo, hi, nx = t0[:, :WIN], t0[:, WIN:], t1[:, :WIN]
                for w, (a, c) in enumerate(((lo, hi), (hi, nx))):
                    tile = jnp.where(low, c, a).reshape(2 * WIN, width)
                    start = pl.multiple_of((2 * pair + w) * AREA + 16 * rows, 16)
                    if array == 0:
                        mean = jnp.mean(tile, axis=-1, keepdims=True)
                        centred = tile - mean
                        inverse = lax.rsqrt(
                            jnp.mean(centred * centred, axis=-1, keepdims=True) + 1e-05
                        )
                        normed = centred * inverse
                        xh_s[pl.ds(start, 16)] = normed
                        xb_s[pl.ds(start, 16)] = normed.astype(BF16)
                        inv_s[pl.ds(start, 16)] = jnp.broadcast_to(inverse, (16, 128))
                    else:
                        keep = r["kept"][myself, WIN * i + 2 * m + w].astype(F32)
                        stash_g[pl.ds(pl.multiple_of(first + start, 16), 16)] = (
                            tile * keep
                        ).astype(BF16)
            return 0

        lax.fori_loop(0, 8, normalise, 0)
        xb = xb_s[...]
        stash_xt[:, pl.ds(first, BATCH)] = xb.T
        for n in range(3):
            qkv_s[:, n * width : (n + 1) * width] = dot(
                xb, wqkv[:, n * width : (n + 1) * width]
            ).astype(BF16)
        dat_s[...] = dot(stash_g[pl.ds(first, BATCH)], wp[...], NT).astype(BF16)

        def attend(w, _):
            j = 4 * half + w
            last_row = jnp.where(row == nrow - 1, i, 0)
            last_col = jnp.where(col == ncol - 1, j // 7, 0)
            bias = jnp.where(row_differs * last_row + col_differs * last_col > 0, -100.0, 0.0)
            rows = pl.ds(pl.multiple_of(w * AREA, AREA), AREA)
            out_rows = pl.ds(pl.multiple_of(first + w * AREA, AREA), AREA)
            for g in range(groups):
                lanes = slice(g * GROUP, (g + 1) * GROUP)

                def part(n):
                    return slice(n * width + g * GROUP, n * width + (g + 1) * GROUP)

                q, k, v = qkv_s[rows, part(0)], qkv_s[rows, part(1)], qkv_s[rows, part(2)]
                spread_q, spread_d = spread(q), spread(dat_s[rows, lanes])
                scores = dot(k, spread_q, NT) * scale + bias
                expo = jnp.exp(scores - jnp.max(scores, axis=0, keepdims=True))
                probs = expo * (1.0 / jnp.sum(expo, axis=0, keepdims=True))
                pb = probs.astype(BF16)
                d_p = dot(v, spread_d, NT)
                delta = jnp.sum(probs * d_p, axis=0, keepdims=True)
                d_s = (probs * (d_p - delta) * scale).astype(BF16)
                att_s[rows, lanes] = gather_heads(dot(pb, v, TN)).astype(BF16)
                stash_d[out_rows, part(0)] = gather_heads(dot(d_s, k, TN)).astype(BF16)
                stash_d[out_rows, part(1)] = dot(d_s, spread_q).astype(BF16)
                stash_d[out_rows, part(2)] = dot(pb, spread_d).astype(BF16)
            return 0

        lax.fori_loop(0, 4, attend, 0)
        stash_at[:, pl.ds(first, BATCH)] = att_s[...].T
        r["dxh"][...] = dot(stash_d[pl.ds(first, BATCH)], wqkv[...], NT)

        def finish(n, _):
            pair, at_row = n // WIN, n % WIN
            tiles = []
            for w in (0, 1):
                here = pl.ds(pl.multiple_of((2 * pair + w) * AREA + WIN * at_row, WIN), WIN)
                grad, normed = r["dxh"][here], xh_s[here]
                inverse = inv_s[here][:, :1]
                tiles.append(
                    inverse
                    * (
                        grad
                        - jnp.mean(grad, axis=-1, keepdims=True)
                        - normed * jnp.mean(grad * normed, axis=-1, keepdims=True)
                    )
                )
            where = pl.ds(pl.multiple_of(32 * half + 16 * pair, 16), 16)
            br[HALF + WIN * i + at_row, where] = jnp.concatenate(tiles, axis=0).astype(BF16)
            r["last"][at_row] = tiles[1]
            return 0

        lax.fori_loop(0, 2 * WIN, finish, 0)

        @pl.when(half == 1)
        def _():
            last = r["last"][...]
            packed = [
                jnp.where(low, last[2 * n], swap_halves(last[2 * n + 1])) for n in range(WIN // 2)
            ]
            edge_ret[pl.ds(pl.multiple_of(32 * i, 32), 32)] = jnp.concatenate(
                packed, axis=0
            ).astype(BF16)

        @pl.when(b == 2)
        def _():
            col_back.start()
            corner_back.start()
            row_back(1).start()

        return 0

    lax.fori_loop(0, 4, batch, 0)
    row_back(0).start()

    share = width // (nrow * ncol)
    span = 8 * share

    part_a, part_b = r["part_a"], r["part_b"]

    def grads_a(step):
        target = (x_at + step) % 4
        lhs = stash_xt[pl.ds(pl.multiple_of(target * span, 16), span), :]
        first = dot(lhs, stash_d[:, :width])
        second = dot(lhs, stash_d[:, width : 2 * width])
        for z in range(2):
            for y in range(4):
                rows = slice((4 * z + y) * share, (4 * z + y + 1) * share)
                part_a[target, z, y] = jnp.concatenate([first[rows], second[rows]], axis=0).astype(
                    BF16
                )

    def grads_b(x, _):
        here = pl.ds(pl.multiple_of(x * span, 16), span)
        first = dot(stash_xt[here, :], stash_d[:, 2 * width :])
        second = dot(stash_at[here, :], stash_g[...])
        for z in range(2):
            for y in range(4):
                rows = slice((4 * z + y) * share, (4 * z + y + 1) * share)
                part_b[y, z, x] = jnp.concatenate([first[rows], second[rows]], axis=0).astype(BF16)
        return 0

    class Ring:
        def __init__(self, base, part, me, forward, backward, relay, direct):
            self.part, self.me, self.relay, self.direct = part, me, relay, direct
            ahead, behind, across = (me + 1) % 4, (me + 3) % 4, (me + 2) % 4
            self.ahead, self.behind = ahead, behind
            self.relay_back = send(base, part.at[across, 0], relay.at[0], backward)
            self.relay_on = send(base + 1, part.at[across, 1], relay.at[1], forward)
            self.own_on = send(base + 2, part.at[ahead, 0], direct.at[0, 0], forward)
            self.own_back = send(base + 3, part.at[behind, 1], direct.at[1, 1], backward)
            self.sum_back = send(base + 4, part.at[behind, 0], direct.at[1, 0], backward)
            self.sum_on = send(base + 5, part.at[ahead, 1], direct.at[0, 1], forward)

        def begin(self):
            self.relay_back.start()
            self.relay_on.start()

        def go_on(self):
            self.own_on.start()
            self.own_back.start()

        def pass_on(self):
            for n, copy, relayed, target in (
                (0, self.sum_back, self.relay_back, self.behind),
                (1, self.sum_on, self.relay_on, self.ahead),
            ):
                relayed.wait_recv()
                total = self.part[target, n].astype(F32) + self.relay[n].astype(F32)
                self.part[target, n] = total.astype(BF16)
                copy.start()

        def arrive(self):
            for copy in (self.own_on, self.own_back, self.sum_back, self.sum_on):
                copy.wait_recv()

        def total(self, z):
            return (
                self.part[self.me, z].astype(F32)
                + self.direct[0, z].astype(F32)
                + self.direct[1, z].astype(F32)
            )

        def close(self):
            for copy in (
                self.relay_back, self.relay_on, self.own_on,
                self.own_back, self.sum_back, self.sum_on,
            ):
                copy.wait_send()

    on_x, back_x, on_y, back_y = at(2, 0), at(-2, 0), at(0, 1), at(0, -1)
    next_a, next_b = r["next_a"], r["next_b"]
    ring_a = Ring(10, part_a, x_at, on_x, back_x, r["relay_a"], r["direct_a"])
    ring_b = Ring(16, part_b, col, on_y, back_y, r["relay_b"], r["direct_b"])
    ring_c = Ring(22, next_a, col, on_y, back_y, r["relay_c"], r["direct_c"])
    ring_d = Ring(28, next_b, x_at, on_x, back_x, r["relay_d"], r["direct_d"])

    grads_a(2)
    ring_a.begin()
    lax.fori_loop(0, 4, grads_b, 0)
    ring_b.begin()
    ring_b.go_on()
    grads_a(1)
    grads_a(3)
    ring_a.go_on()
    ring_a.pass_on()
    ring_b.pass_on()
    grads_a(0)

    col_back.wait_recv()
    corner_back.wait_recv()
    row_back(0).wait_recv()
    row_back(1).wait_recv()

    def add_branch(k, _):
        left = left_in[pl.ds(pl.multiple_of(16 * k, 16), 16)].astype(F32)
        for n in range(4):
            at_row = 4 * k + n
            tile = left[WIN * (n // 2) : WIN * (n // 2 + 1)]
            before = swap_halves(tile) if n % 2 else tile
            for m in range(tile_cols // 16):
                here = slice(16 * m, 16 * m + 16)
                both = br[at_row, here].astype(F32)
                lo, hi = both[:WIN], both[WIN:]
                grad = jnp.concatenate(
                    [jnp.where(low, before, lo), jnp.where(low, lo, hi)], axis=0
                )
                before = hi
                r["out"][at_row, here] = (xg[1, at_row, here].astype(F32) + grad).astype(BF16)
        return 0

    lax.fori_loop(0, tile_rows // 4, add_branch, 0)

    ring_a.arrive()
    for z in range(2):
        total = ring_a.total(z).astype(BF16)
        for y in range(4):
            next_a[y, z] = total[y]
    ring_c.begin()
    ring_c.go_on()
    ring_b.arrive()
    for z in range(2):
        total = ring_b.total(z).astype(BF16)
        for x in range(4):
            next_b[x, z] = total[x]
    ring_d.begin()
    ring_d.go_on()
    ring_c.pass_on()
    ring_d.pass_on()

    across = at(z_across, 0)
    last_out, last_in, mine = r["last_out"], r["last_in"], r["mine"]
    crossing = []
    for n, ring in enumerate((ring_c, ring_d)):
        ring.arrive()
        last_out[n] = ring.total(1 - z_at).astype(BF16)
        copy = send(34 + n, last_out.at[n], last_in.at[n], across)
        copy.start()
        crossing.append(copy)
        mine[n] = ring.total(z_at)
    for n, copy in enumerate(crossing):
        copy.wait_recv()
        total = mine[n] + last_in[n].astype(F32)
        if n == 0:
            r["qkv_grad"][:, :width] = total[:share]
            r["qkv_grad"][:, width : 2 * width] = total[share:]
        else:
            r["qkv_grad"][:, 2 * width :] = total[:share]
            r["proj_grad"][...] = total[share:]

    for array in (0, 1):
        for half in (0, 1):
            row_halo(array, half).wait_send()
    for copy in (col_halo, corner, col_back, corner_back, row_back(0), row_back(1), *crossing):
        copy.wait_send()
    for ring in (ring_a, ring_b, ring_c, ring_d):
        ring.close()


def on_device(scene, cotangent, query_key_value_weight, proj_weight, kept):
    rows, cols, width = scene.shape
    share = width // 32
    both = 2 * share
    tokens = rows * HALF
    all_tokens = rows * cols
    vmem = {
        "xg": ((2, rows + HALF, cols + 16, width), BF16),
        "br": ((rows + HALF, cols, width), BF16),
        "stash_d": ((all_tokens, 3 * width), BF16),
        "stash_g": ((all_tokens, width), BF16),
        "stash_xt": ((width, all_tokens), BF16),
        "stash_at": ((width, all_tokens), BF16),
        "xb": ((BATCH, width), BF16),
        "xh": ((BATCH, width), F32),
        "inv": ((BATCH, 128), F32),
        "qkv": ((BATCH, 3 * width), BF16),
        "dat": ((BATCH, width), BF16),
        "att": ((BATCH, width), BF16),
        "dxh": ((BATCH, width), F32),
        "last": ((WIN, WIN, width), F32),
        "wqkv": ((width, 3 * width), BF16),
        "wp": ((width, width), BF16),
        "edge_f": ((2, tokens, width), F32),
        "edge_out": ((2, tokens, width), BF16),
        "edge_in": ((2, tokens, width), BF16),
        "edge_ret": ((tokens, width), BF16),
        "left_in": ((tokens, width), BF16),
        "part_a": ((4, 2, 4, both, width), BF16),
        "part_b": ((4, 2, 4, both, width), BF16),
        "relay_a": ((2, 4, both, width), BF16),
        "relay_b": ((2, 4, both, width), BF16),
        "direct_a": ((2, 2, 4, both, width), BF16),
        "direct_b": ((2, 2, 4, both, width), BF16),
        "next_a": ((4, 2, both, width), BF16),
        "next_b": ((4, 2, both, width), BF16),
        "relay_c": ((2, both, width), BF16),
        "relay_d": ((2, both, width), BF16),
        "direct_c": ((2, 2, both, width), BF16),
        "direct_d": ((2, 2, both, width), BF16),
        "last_out": ((2, both, width), BF16),
        "last_in": ((2, both, width), BF16),
        "mine": ((2, both, width), F32),
    }
    sems = {
        "load_sems": pltpu.SemaphoreType.DMA((4,)),
        "send_sems": pltpu.SemaphoreType.DMA((36,)),
        "recv_sems": pltpu.SemaphoreType.DMA((36,)),
    }
    names = (
        ["scene", "cotangent", "wqkv_hbm", "wp_hbm", "kept", "out", "qkv_grad", "proj_grad"]
        + list(vmem)
        + list(sems)
    )
    anywhere = pl.BlockSpec(memory_space=pl.ANY)
    in_vmem = pl.BlockSpec(memory_space=pltpu.VMEM)
    return pl.pallas_call(
        functools.partial(kernel, names),
        out_shape=(
            jax.ShapeDtypeStruct((rows, cols, width), BF16),
            jax.ShapeDtypeStruct((share, 3 * width), F32),
            jax.ShapeDtypeStruct((share, width), F32),
        ),
        in_specs=[anywhere] * 4 + [pl.BlockSpec(memory_space=pltpu.SMEM)],
        out_specs=(in_vmem,) * 3,
        scratch_shapes=[pltpu.VMEM(*spec) for spec in vmem.values()] + list(sems.values()),
        compiler_params=pltpu.CompilerParams(
            collective_id=0, has_side_effects=True, vmem_limit_bytes=60 * 1024 * 1024
        ),
    )(scene, cotangent, query_key_value_weight, proj_weight, kept)


def solution(mesh):
    return jax.shard_map(
        on_device,
        mesh=mesh,
        in_specs=(
            P(("scene", "row"), "col", None),
            P(("scene", "row"), "col", None),
            P(),
            P(),
            P("scene", None),
        ),
        out_specs=(
            P(("scene", "row"), "col", None),
            P(("scene", "row", "col"), None),
            P(("scene", "row", "col"), None),
        ),
        check_vma=False,
    )
```

time: 663 us -> 128 us (0.19)
  waiting for transfers between devices: 467 us -> 0 us
  Pallas kernels: 0 us -> 122 us
  matrix products: 89.9 us -> 0 us
  local copies, waits for them, and re-layouts: 52 us -> 5.44 us
  other arithmetic: 19.7 us -> 0 us
  starting transfers between devices: 18.4 us -> 0 us
  between operations: 14.2 us -> 0.66 us
    reduce_scatter x2 -> x0, waiting for transfers between devices: 419 us -> none  [the longest x1 277 us: on_device(): lax.psum_scatter(qkv_part, ('row', 'col'), scatter_dimension=0, tiled=True)]
    pallas_call x0 -> x1, Pallas kernels: none -> 122 us  [on_device(): pl.pallas_call(functools.partial(kernel, names), out_shape=(jax.ShapeDtyp...]
    dot_general x10 -> x0, matrix products: 79.4 us -> none  [the longest x1 17.2 us: window_grads(): jnp.einsum('nhqk,nqhc->nkhc', d_s, query, preferred_element_type=single_p...]
    ppermute x4 -> x0, waiting for transfers between devices: 47.9 us -> none  [shifted(): return lax.ppermute(block, axis, route)]
    slice x9 -> x0, local copies, waits for them, and re-layouts: 19.4 us -> none  [the longest x2 5.61 us: window_grads(): values = qkv[:, :, 2 * width:].reshape(count, area, heads, HD)]
    ppermute x4 -> x0, starting transfers between devices: 18.1 us -> none  [shifted(): return lax.ppermute(block, axis, route)]
    reshape x3 -> x0, local copies, waits for them, and re-layouts: 11.5 us -> none  [the longest x1 3.85 us: window_grads(): d_q.reshape(count, area, width)]
    sub x1 -> x0, matrix products: 10.5 us -> none  [window_grads(): expo = jnp.exp(scores - top)]
  transfers between devices with their start and end apart: 6 -> 0, of which waited for: 6 -> 0; matrix products, arithmetic and copies ran while one was open for 16% -> 0% of each run, Pallas kernels for 0% -> 0%
where the time goes in v1:
time: 128 us
  Pallas kernels  122 us (95%)
  local copies, waits for them, and re-layouts  5.44 us (4%)
    pallas_call x1, Pallas kernels, on_device(): pl.pallas_call(functools.partial(kernel, names), out_shape=(jax.ShapeDtyp...  122 us
    unnamed x8, local copies, waits for them, and re-layouts  5.44 us

profile of v1, /device:TPU:32, one launch (start us, length us, event | category | flops | bytes accessed | tf_op | source)
XLA Modules:
  0.0 128.0 jit_solution(12515766896165086320)
XLA Ops:
  0.6 1.4 %copy.8.refs_4_ = s32[32,16]{1,0:T(8,128)} copy(s32[32,16]{0,1:T(8,128)} %param.9) | data formatting | bytes 4096 | tf_op args[4]
  2.0 121.9 %shard_map.76 = (bf16[16,64,768]{2,1,0:T(8,128)(2,1)}, f32[24,2304]{1,0:T(8,128)}, f32[24,768]{1,0:T(8,128)}) custom-call(bf16[16,64,768]{2,1,0:T(8,128)(2,1)} %refs_0_.1, bf16[16,64,768]{2,1,0:T(8,128)(2,1)} %refs_1_.1, bf16[768,2304]{1,0:T(8,128)(2,1)} %refs_2_.1, bf16[768,768]{1,0:T(8,128)(2,1)} %refs_3_.1, s32[32,16]{1,0:T(8,128)} %copy.8.refs_4_), custom_call_target="tpu_custom_call" | custom-call | tf_op jit(solution)/shard_map/pallas_call | solution.py:537
  123.9 0.0 copy-start
  123.9 0.0 copy-start.1
  123.9 2.7 %copy.12 = bf16[16,64,768]{2,1,0:T(8,128)(2,1)} copy(bf16[16,64,768]{2,1,0:T(8,128)(2,1)} %get-tuple-element.6) | data formatting | bytes 3145728
  126.7 0.0 copy-done
  126.7 0.7 copy.13
  127.4 0.0 copy-done.1
  127.4 0.6 copy.14
Async XLA Ops:
  123.9 2.8 %copy-start = (f32[24,2304]{1,0:T(8,128)S(1)}, f32[24,2304]{1,0:T(8,128)}, u32[]{:S(2)}) copy-start(f32[24,2304]{1,0:T(8,128)} %get-tuple-element.7) | copy-start | bytes 663556
  123.9 3.4 %copy-start.1 = (f32[24,768]{1,0:T(8,128)S(1)}, f32[24,768]{1,0:T(8,128)}, u32[]{:S(2)}) copy-start(f32[24,768]{1,0:T(8,128)} %get-tuple-element.8) | copy-start | bytes 221188

commit v2 on v1

v2 whole, which is shorter than its diff:
```python
import functools

import jax
import jax.numpy as jnp
from jax import lax
from jax.experimental import pallas as pl
from jax.experimental.pallas import tpu as pltpu
from jax.sharding import PartitionSpec as P

HD = 32
WIN = 8
HALF = 4
AREA = 64
PACK = 4
GROUP = PACK * HD
BATCH = 2 * AREA
F32 = jnp.float32
BF16 = jnp.bfloat16
NT = (((1,), (1,)), ((), ()))
TN = (((0,), (0,)), ((), ()))


def dot(a, b, dims=(((1,), (0,)), ((), ()))):
    return lax.dot_general(a, b, dims, preferred_element_type=F32)


def swap_halves(tile):
    return pltpu.roll(tile, HALF, tile.ndim - 2)


def kernel(names, *refs):
    r = dict(zip(names, refs))
    scene, cot = r["scene"], r["cotangent"]
    xg, br, stash_d, stash_g = r["xg"], r["br"], r["stash_d"], r["stash_g"]
    stash_xt, stash_at = r["stash_xt"], r["stash_at"]
    xb_s, xh_s, inv_s, qkv_s, dat_s, att_s = (
        r["xb"], r["xh"], r["inv"], r["qkv"], r["dat"], r["att"],
    )
    wqkv, wp = r["wqkv"], r["wp"]
    tile_rows, tile_cols, width = scene.shape
    groups = width // GROUP
    pairs = tile_cols // 16
    row, col = lax.axis_index("row"), lax.axis_index("col")
    nrow, ncol = lax.axis_size("row"), lax.axis_size("col")
    x_at, z_at = row // 2, row % 2
    myself = row * ncol + col

    def at(drow, dcol):
        return {"row": (row + drow + nrow) % nrow, "col": (col + dcol + ncol) % ncol}

    def send(number, src, dst, device):
        return pltpu.make_async_remote_copy(
            src_ref=src,
            dst_ref=dst,
            send_sem=r["send_sems"].at[number],
            recv_sem=r["recv_sems"].at[number],
            device_id=device,
            device_id_type=pl.DeviceIdType.MESH,
        )

    barrier = pltpu.get_barrier_semaphore()
    partners = [(-1, 0), (1, 0), (0, -1), (0, 1), (2, 0), (-2, 0)]
    for partner in partners:
        pl.semaphore_signal(
            barrier, inc=1, device_id=at(*partner), device_id_type=pl.DeviceIdType.MESH
        )

    own = pl.ds(0, tile_rows)
    loads = [
        pltpu.make_async_copy(src, dst, r["load_sems"].at[k])
        for k, (src, dst) in enumerate(
            [
                (scene, xg.at[0, own, pl.ds(0, tile_cols)]),
                (cot, xg.at[1, own, pl.ds(0, tile_cols)]),
                (r["wqkv_hbm"], wqkv),
                (r["wp_hbm"], wp),
            ]
        )
    ]
    for load in loads:
        load.start()

    def row_halo(array, m):
        src = (scene, cot)[array]
        columns = pl.ds(m * 16, 16)
        return send(
            2 * m + array,
            src.at[pl.ds(0, HALF), columns],
            xg.at[array, pl.ds(tile_rows, HALF), columns],
            at(-1, 0),
        )

    low = lax.broadcasted_iota(jnp.int32, (WIN, width), 0) < HALF

    loads[0].wait()
    loads[1].wait()

    def pack_columns(k, _):
        for array in (0, 1):
            pair = xg[array, pl.ds(2 * k, 2), pl.ds(0, 16)].astype(F32)[:, :WIN]
            tile = jnp.where(low, pair[0], swap_halves(pair[1]))
            r["edge_f"][array, pl.ds(pl.multiple_of(k * WIN, WIN), WIN)] = tile
        return 0

    lax.fori_loop(0, tile_rows // 2, pack_columns, 0)
    r["edge_out"][...] = r["edge_f"][...].astype(BF16)

    edge_in, corner_in = r["edge_in"], r["corner_in"]
    tokens = tile_rows * HALF
    col_halo = send(8, r["edge_out"], edge_in, at(0, -1))
    corner = send(9, edge_in.at[:, pl.ds(0, 16)], corner_in, at(-1, 0))
    pl.semaphore_wait(barrier, len(partners))
    for m in (3, 2):
        for array in (0, 1):
            row_halo(array, m).start()
    col_halo.start()

    def unpack_columns(source, start, first_row, count):
        def body(k, _):
            for array in (0, 1):
                both = source[array, pl.ds(pl.multiple_of(start + k * 16, 16), 16)].astype(F32)
                for n in (0, 1):
                    tile = both[n * WIN : (n + 1) * WIN]
                    for odd in (0, 1):
                        part = swap_halves(tile) if odd else tile
                        whole = jnp.concatenate([part, jnp.zeros_like(part)], axis=0)
                        xg[array, first_row + 4 * k + 2 * n + odd, pl.ds(tile_cols, 16)] = (
                            whole.astype(BF16)
                        )
            return 0

        lax.fori_loop(0, count, body, 0)

    for load in loads[2:]:
        load.wait()
    wqkv_t, wp_t = r["wqkv_t"], r["wp_t"]
    for n in range(3):
        wqkv_t[n * width : (n + 1) * width] = wqkv[:, n * width : (n + 1) * width].T
    wp_t[...] = wp[...].T

    edge_ret, left_in, corner_mid = r["edge_ret"], r["left_in"], r["corner_mid"]
    col_back = send(
        10, edge_ret.at[pl.ds(0, tokens - 16)], left_in.at[pl.ds(16, tokens - 16)], at(0, 1)
    )
    corner_down = send(11, edge_ret.at[pl.ds(tokens - 16, 16)], corner_mid, at(1, 0))
    corner_right = send(12, corner_mid, left_in.at[pl.ds(0, 16)], at(0, 1))
    row_back = send(
        13, br.at[pl.ds(tile_rows, HALF)], br.at[pl.ds(0, HALF)], at(1, 0)
    )

    scale = HD ** (-0.5)
    lane_head = lax.broadcasted_iota(jnp.int32, (AREA, GROUP), 1) // HD
    key_at = lax.broadcasted_iota(jnp.int32, (AREA, PACK * AREA), 0)
    query_at = lax.broadcasted_iota(jnp.int32, (AREA, PACK * AREA), 1) % AREA
    row_differs = jnp.where(key_at // 32 != query_at // 32, 1, 0)
    col_differs = jnp.where((key_at % 8) // 4 != (query_at % 8) // 4, 1, 0)

    def spread(block):
        zero = jnp.zeros_like(block)
        return jnp.concatenate([jnp.where(lane_head == h, block, zero) for h in range(PACK)], axis=0)

    def gather_heads(full):
        total = full[:AREA]
        for h in range(1, PACK):
            total = jnp.where(lane_head == h, full[h * AREA : (h + 1) * AREA], total)
        return total

    grads = r["grads"]
    early = 6 * BATCH

    def gather_early(x, _):
        here = pl.ds(pl.multiple_of(x * (width // 4), 16), width // 4)
        for q in range(4):
            lhs = (stash_at if q == 3 else stash_xt)[here, :early]
            rhs = stash_g[:early] if q == 3 else stash_d[:early, q * width : (q + 1) * width]
            grads[q, here] = dot(lhs, rhs)
        return 0

    def step(p, _):
        i = p // pairs
        m = p + i * (2 * pairs - 1 - 2 * p)

        @pl.when(p == 2)
        def _():
            col_halo.wait_recv()
            corner.start()
            unpack_columns(edge_in, 16, HALF, (tile_rows - HALF) // 4)

        @pl.when(p == 4)
        def _():
            for array in (0, 1):
                row_halo(array, 3).wait_send()
            for array in (0, 1):
                row_halo(array, 1).start()
            for array in (0, 1):
                row_halo(array, 3).wait_recv()
            corner.wait_recv()
            unpack_columns(corner_in, 0, tile_rows, 1)

        @pl.when(p == 5)
        def _():
            col_back.start()
            for array in (0, 1):
                row_halo(array, 2).wait_send()
            for array in (0, 1):
                row_halo(array, 0).start()
            for array in (0, 1):
                row_halo(array, 2).wait_recv()

        @pl.when(p == 6)
        def _():
            lax.fori_loop(0, 4, gather_early, 0)
            for array in (0, 1):
                row_halo(array, 1).wait_recv()

        @pl.when(p == 7)
        def _():
            for array in (0, 1):
                row_halo(array, 0).wait_recv()

        first = pl.multiple_of(p * BATCH, BATCH)
        here = pl.ds(pl.multiple_of(16 * m, 16), 16)
        following = pl.ds(pl.multiple_of(16 * m + 16, 16), 16)
        keep = [r["kept"][WIN * i + 2 * m + w, myself].astype(F32) for w in range(2)]
        for rows in range(4):
            top = pl.ds(WIN * i + HALF + 2 * rows, 2)
            for array in (0, 1):
                t0 = xg[array, top, here].astype(F32)
                t1 = xg[array, top, following].astype(F32)
                lo, hi, nx = t0[:, :WIN], t0[:, WIN:], t1[:, :WIN]
                for w, (a, c) in enumerate(((lo, hi), (hi, nx))):
                    tile = jnp.where(low, c, a).reshape(2 * WIN, width)
                    start = w * AREA + 16 * rows
                    if array == 0:
                        mean = jnp.mean(tile, axis=-1, keepdims=True)
                        centred = tile - mean
                        inverse = lax.rsqrt(
                            jnp.mean(centred * centred, axis=-1, keepdims=True) + 1e-05
                        )
                        normed = centred * inverse
                        xh_s[start : start + 16] = normed
                        xb_s[start : start + 16] = normed.astype(BF16)
                        inv_s[start : start + 16] = jnp.broadcast_to(inverse, (16, 128))
                    else:
                        stash_g[pl.ds(pl.multiple_of(first + start, 16), 16)] = (
                            tile * keep[w]
                        ).astype(BF16)

        xb = xb_s[...]
        stash_xt[:, pl.ds(first, BATCH)] = xb.T
        for n in range(3):
            qkv_s[:, n * width : (n + 1) * width] = dot(
                xb, wqkv[:, n * width : (n + 1) * width]
            ).astype(BF16)
        dat_s[...] = dot(stash_g[pl.ds(first, BATCH)], wp_t[...]).astype(BF16)

        last_row = jnp.where(row == nrow - 1, i, 0)
        last_col = jnp.where(col == ncol - 1, m // (pairs - 1), 0)
        biases = [
            jnp.where(row_differs * last_row + col_differs * lc > 0, -100.0, 0.0)
            for lc in (0, last_col)
        ]

        def part(n, g):
            return slice(n * width + g * GROUP, n * width + (g + 1) * GROUP)

        units = [(w, g) for w in range(2) for g in range(groups)]
        near = [slice(w * AREA, (w + 1) * AREA) for w in range(2)]
        far = [pl.ds(pl.multiple_of(first + w * AREA, AREA), AREA) for w in range(2)]
        q, k, v = [[qkv_s[near[w], part(n, g)] for w, g in units] for n in range(3)]
        spread_q = [spread(block) for block in q]
        spread_d = [spread(dat_s[near[w], part(0, g)]) for w, g in units]
        scores = [
            dot(a, c, NT) * scale + biases[w] for (w, _), a, c in zip(units, k, spread_q)
        ]
        d_p = [dot(a, c, NT) for a, c in zip(v, spread_d)]
        expo = [jnp.exp(a - jnp.max(a, axis=0, keepdims=True)) for a in scores]
        probs = [a * (1.0 / jnp.sum(a, axis=0, keepdims=True)) for a in expo]
        pb = [a.astype(BF16) for a in probs]
        d_s = [
            (a * (c - jnp.sum(a * c, axis=0, keepdims=True)) * scale).astype(BF16)
            for a, c in zip(probs, d_p)
        ]
        attended = [dot(a, c, TN) for a, c in zip(pb, v)]
        d_v = [dot(a, c) for a, c in zip(pb, spread_d)]
        d_q = [dot(a, c, TN) for a, c in zip(d_s, k)]
        d_k = [dot(a, c) for a, c in zip(d_s, spread_q)]
        for n, (w, g) in enumerate(units):
            att_s[near[w], part(0, g)] = gather_heads(attended[n]).astype(BF16)
            stash_d[far[w], part(0, g)] = gather_heads(d_q[n]).astype(BF16)
            stash_d[far[w], part(1, g)] = d_k[n].astype(BF16)
            stash_d[far[w], part(2, g)] = d_v[n].astype(BF16)

        stash_at[:, pl.ds(first, BATCH)] = att_s[...].T
        r["dxh"][...] = dot(stash_d[pl.ds(first, BATCH)], wqkv_t[...])

        last = []
        for at_row in range(WIN):
            tiles = []
            for w in (0, 1):
                near_row = slice(w * AREA + WIN * at_row, w * AREA + WIN * (at_row + 1))
                grad, normed = r["dxh"][near_row], xh_s[near_row]
                inverse = inv_s[near_row][:, :1]
                tiles.append(
                    inverse
                    * (
                        grad
                        - jnp.mean(grad, axis=-1, keepdims=True)
                        - normed * jnp.mean(grad * normed, axis=-1, keepdims=True)
                    )
                )
            br[HALF + WIN * i + at_row, here] = jnp.concatenate(tiles, axis=0).astype(BF16)
            r["last"][at_row] = tiles[1]

        @pl.when(m == pairs - 1)
        def _():
            last = r["last"][...]
            packed = [
                jnp.where(low, last[2 * n], swap_halves(last[2 * n + 1])) for n in range(WIN // 2)
            ]
            edge_ret[pl.ds(pl.multiple_of(32 * i, 32), 32)] = jnp.concatenate(
                packed, axis=0
            ).astype(BF16)

        return 0

    lax.fori_loop(0, 2 * pairs, step, 0)
    corner_down.start()
    row_back.start()

    share = width // (nrow * ncol)
    parts = [r["part_%d" % q] for q in range(4)]

    def close_grads(q):
        def body(x, _):
            here = pl.ds(pl.multiple_of(x * (width // 4), 16), width // 4)
            lhs = (stash_at if q == 3 else stash_xt)[here, early:]
            rhs = stash_g[early:] if q == 3 else stash_d[early:, q * width : (q + 1) * width]
            block = grads[q, here] + dot(lhs, rhs)
            for z in range(2):
                for y in range(4):
                    piece = block[(4 * z + y) * share : (4 * z + y + 1) * share]
                    piece = jnp.concatenate(
                        [piece[:, : width // 2], piece[:, width // 2 :]], axis=0
                    ).astype(BF16)
                    if q < 2:
                        parts[q][x, z, y] = piece
                    else:
                        parts[q][y, z, x] = piece
            return 0

        lax.fori_loop(0, 4, body, 0, unroll=4)

    class Ring:
        def __init__(self, base, part, me, forward, backward, relay, direct):
            self.part, self.me, self.relay, self.direct = part, me, relay, direct
            ahead, behind, across = (me + 1) % 4, (me + 3) % 4, (me + 2) % 4
            self.ahead, self.behind = ahead, behind
            self.relay_back = send(base, part.at[across, 0], relay.at[0], backward)
            self.relay_on = send(base + 1, part.at[across, 1], relay.at[1], forward)
            self.own_on = send(base + 2, part.at[ahead, 0], direct.at[0, 0], forward)
            self.own_back = send(base + 3, part.at[behind, 1], direct.at[1, 1], backward)
            self.sum_back = send(base + 4, part.at[behind, 0], direct.at[1, 0], backward)
            self.sum_on = send(base + 5, part.at[ahead, 1], direct.at[0, 1], forward)

        def begin(self):
            self.relay_back.start()
            self.relay_on.start()

        def go_on(self):
            self.own_on.start()
            self.own_back.start()

        def pass_on(self):
            for n, copy, relayed, target in (
                (0, self.sum_back, self.relay_back, self.behind),
                (1, self.sum_on, self.relay_on, self.ahead),
            ):
                relayed.wait_recv()
                total = self.part[target, n].astype(F32) + self.relay[n].astype(F32)
                self.part[target, n] = total.astype(BF16)
                copy.start()

        def arrive(self):
            for copy in (self.own_on, self.own_back, self.sum_back, self.sum_on):
                copy.wait_recv()

        def total(self, z):
            return (
                self.part[self.me, z].astype(F32)
                + self.direct[0, z].astype(F32)
                + self.direct[1, z].astype(F32)
            )

        def close(self):
            for copy in (
                self.relay_back, self.relay_on, self.own_on,
                self.own_back, self.sum_back, self.sum_on,
            ):
                copy.wait_send()

    on_x = (x_at, at(2, 0), at(-2, 0))
    on_y = (col, at(0, 1), at(0, -1))
    outer, inner = [], []
    for q in range(4):
        axes = (on_x, on_y) if q < 2 else (on_y, on_x)
        for rings, name, axis, base in (
            (outer, "part_%d", axes[0], 16),
            (inner, "next_%d", axes[1], 40),
        ):
            rings.append(
                Ring(
                    base + 6 * q,
                    r[name % q],
                    *axis,
                    r["relay_" + name % q],
                    r["direct_" + name % q],
                )
            )

    def turn(q):
        outer[q].arrive()
        for z in range(2):
            total = outer[q].total(z).astype(BF16)
            for n in range(4):
                inner[q].part[n, z] = total[n]
        inner[q].begin()
        inner[q].go_on()

    last_out, last_in, mine = r["last_out"], r["last_in"], r["mine"]
    crossing = [send(64 + q, last_out.at[q], last_in.at[q], at(1 - 2 * z_at, 0)) for q in range(4)]

    def cross(q):
        inner[q].arrive()
        last_out[q] = inner[q].total(1 - z_at).astype(BF16)
        crossing[q].start()
        mine[q] = inner[q].total(z_at)

    def place(k, _):
        left = left_in[pl.ds(pl.multiple_of(16 * k, 16), 16)].astype(F32)
        for n in range(4):
            at_row = 4 * k + n
            tile = left[WIN * (n // 2) : WIN * (n // 2 + 1)]
            before = swap_halves(tile) if n % 2 else tile
            for m in range(pairs):
                here = slice(16 * m, 16 * m + 16)
                both = br[at_row, here].astype(F32)
                lo, hi = both[:WIN], both[WIN:]
                r["out"][at_row, here] = jnp.concatenate(
                    [jnp.where(low, before, lo), jnp.where(low, lo, hi)], axis=0
                ).astype(BF16)
                before = hi
        return 0

    order = (0, 2, 1, 3)
    for q in order:
        close_grads(q)
        outer[q].begin()
        outer[q].go_on()
    for q in order:
        outer[q].pass_on()
    col_back.wait_recv()
    lax.fori_loop(1, tile_rows // 4, place, 0)
    for q in order:
        turn(q)
    corner_down.wait_recv()
    corner_right.start()
    for q in order:
        inner[q].pass_on()
    row_back.wait_recv()
    corner_right.wait_recv()
    lax.fori_loop(0, 1, place, 0)
    for q in order:
        cross(q)
    for q in (0, 2, 1, 3):
        crossing[q].wait_recv()
        total = mine[q] + last_in[q].astype(F32)
        total = jnp.concatenate([total[:share], total[share:]], axis=1)
        if q < 3:
            r["qkv_grad"][:, q * width : (q + 1) * width] = total
        else:
            r["proj_grad"][...] = total

    for array in (0, 1):
        for m in (1, 0):
            row_halo(array, m).wait_send()
    for copy in (col_halo, corner, col_back, corner_down, corner_right, row_back, *crossing):
        copy.wait_send()
    for ring in (*outer, *inner):
        ring.close()


def on_device(scene, cotangent, query_key_value_weight, proj_weight, kept):
    rows, cols, width = scene.shape
    share = width // 32
    piece = (2 * share, width // 2)
    tokens = rows * HALF
    all_tokens = rows * cols
    vmem = {
        "xg": ((2, rows + HALF, cols + 16, width), BF16),
        "br": ((rows + HALF, cols, width), BF16),
        "stash_d": ((all_tokens, 3 * width), BF16),
        "stash_g": ((all_tokens, width), BF16),
        "stash_xt": ((width, all_tokens), BF16),
        "stash_at": ((width, all_tokens), BF16),
        "grads": ((4, width, width), F32),
        "xb": ((BATCH, width), BF16),
        "xh": ((BATCH, width), F32),
        "inv": ((BATCH, 128), F32),
        "qkv": ((BATCH, 3 * width), BF16),
        "dat": ((BATCH, width), BF16),
        "att": ((BATCH, width), BF16),
        "dxh": ((BATCH, width), F32),
        "last": ((WIN, WIN, width), F32),
        "wqkv": ((width, 3 * width), BF16),
        "wp": ((width, width), BF16),
        "wqkv_t": ((3 * width, width), BF16),
        "wp_t": ((width, width), BF16),
        "edge_f": ((2, tokens, width), F32),
        "edge_out": ((2, tokens, width), BF16),
        "edge_in": ((2, tokens, width), BF16),
        "corner_in": ((2, 16, width), BF16),
        "edge_ret": ((tokens, width), BF16),
        "left_in": ((tokens, width), BF16),
        "corner_mid": ((16, width), BF16),
        "last_out": ((4, *piece), BF16),
        "last_in": ((4, *piece), BF16),
        "mine": ((4, *piece), F32),
    }
    for q in range(4):
        vmem["part_%d" % q] = ((4, 2, 4, *piece), BF16)
        vmem["relay_part_%d" % q] = ((2, 4, *piece), BF16)
        vmem["direct_part_%d" % q] = ((2, 2, 4, *piece), BF16)
        vmem["next_%d" % q] = ((4, 2, *piece), BF16)
        vmem["relay_next_%d" % q] = ((2, *piece), BF16)
        vmem["direct_next_%d" % q] = ((2, 2, *piece), BF16)
    sems = {
        "load_sems": pltpu.SemaphoreType.DMA((4,)),
        "send_sems": pltpu.SemaphoreType.DMA((68,)),
        "recv_sems": pltpu.SemaphoreType.DMA((68,)),
    }
    names = (
        ["scene", "cotangent", "wqkv_hbm", "wp_hbm", "kept", "out", "qkv_grad", "proj_grad"]
        + list(vmem)
        + list(sems)
    )
    anywhere = pl.BlockSpec(memory_space=pl.ANY)
    in_vmem = pl.BlockSpec(memory_space=pltpu.VMEM)
    branch, qkv_grad, proj_grad = pl.pallas_call(
        functools.partial(kernel, names),
        out_shape=(
            jax.ShapeDtypeStruct((rows, cols, width), BF16),
            jax.ShapeDtypeStruct((share, 3 * width), F32),
            jax.ShapeDtypeStruct((share, width), F32),
        ),
        in_specs=[anywhere] * 4 + [pl.BlockSpec(memory_space=pltpu.SMEM)],
        out_specs=(in_vmem,) * 3,
        scratch_shapes=[pltpu.VMEM(*spec) for spec in vmem.values()] + list(sems.values()),
        compiler_params=pltpu.CompilerParams(
            collective_id=0, has_side_effects=True, vmem_limit_bytes=60 * 1024 * 1024
        ),
    )(scene, cotangent, query_key_value_weight, proj_weight, kept.T)
    scene_grad = (cotangent.astype(F32) + branch.astype(F32)).astype(BF16)
    return scene_grad, qkv_grad, proj_grad


def solution(mesh):
    return jax.shard_map(
        on_device,
        mesh=mesh,
        in_specs=(
            P(("scene", "row"), "col", None),
            P(("scene", "row"), "col", None),
            P(),
            P(),
            P("scene", None),
        ),
        out_specs=(
            P(("scene", "row"), "col", None),
            P(("scene", "row", "col"), None),
            P(("scene", "row", "col"), None),
        ),
        check_vma=False,
    )
```

time: 128 us -> 100 us (0.78)
  Pallas kernels: 122 us -> 94.3 us
  local copies, waits for them, and re-layouts: 5.44 us -> 1.33 us
  other arithmetic: 0 us -> 3.06 us
    pallas_call x1, Pallas kernels: 122 us -> 94.3 us  [on_device(): pl.pallas_call(functools.partial(kernel, names), out_shape=(jax.ShapeDtyp...]
    unnamed x8, local copies, waits for them, and re-layouts: 5.44 us -> 1.33 us
    convert_element_type x0 -> x1, other arithmetic: none -> 3.06 us  [on_device(): scene_grad = (cotangent.astype(F32) + branch.astype(F32)).astype(BF16)]
where the time goes in v2:
time: 100 us; the launch traced here: 99.3 us
  Pallas kernels  94.3 us (94%)
  other arithmetic  3.06 us (3%)
  local copies, waits for them, and re-layouts  1.33 us (1%)
    pallas_call x1, Pallas kernels, on_device(): pl.pallas_call(functools.partial(kernel, names), out_shape=(jax.ShapeDtyp...  94.3 us
    convert_element_type x1, other arithmetic, on_device(): scene_grad = (cotangent.astype(F32) + branch.astype(F32)).astype(BF16)  3.06 us

profile of v2, /device:TPU:32, one launch (start us, length us, event | category | flops | bytes accessed | tf_op | source)
XLA Modules:
  0.0 99.3 jit_solution(7612164597268251668)
XLA Ops:
  0.6 0.0 copy-start
  0.6 94.3 %shard_map.76 = (bf16[16,64,768]{2,1,0:T(8,128)(2,1)}, f32[24,2304]{1,0:T(8,128)}, f32[24,768]{1,0:T(8,128)}) custom-call(bf16[16,64,768]{2,1,0:T(8,128)(2,1)} %refs_0_.1, bf16[16,64,768]{2,1,0:T(8,128)(2,1)} %refs_1_.1, bf16[768,2304]{1,0:T(8,128)(2,1)} %refs_2_.1, bf16[768,768]{1,0:T(8,128)(2,1)} %refs_3_.1, s32[16,32]{1,0:T(8,128)} %bitcast.1), custom_call_target="tpu_custom_call" | custom-call | tf_op jit(solution)/shard_map/pallas_call | solution.py:549
  94.9 0.0 copy-done
  94.9 0.0 copy-start.1
  94.9 0.0 copy-start.2
  95.0 3.1 %add_convert_fusion = bf16[16,64,768]{2,1,0:T(8,128)(2,1)} fusion(bf16[16,64,768]{2,1,0:T(8,128)(2,1)} %get-tuple-element.6, bf16[16,64,768]{2,1,0:T(8,128)(2,1)S(1)} %copy-done), kind=kLoop, calls=%fused_computation | loop fusion | flops 3145728 | bytes 4718592 | tf_op jit(solution)/shard_map/convert_element_type | solution.py:563
  98.0 0.0 copy-done.1
  98.0 0.7 copy.10
  98.7 0.0 copy-done.2
  98.7 0.6 copy.11
Async XLA Ops:
  0.6 94.3 %copy-start = (bf16[16,64,768]{2,1,0:T(8,128)(2,1)S(1)}, bf16[16,64,768]{2,1,0:T(8,128)(2,1)}, u32[]{:S(2)}) copy-start(bf16[16,64,768]{2,1,0:T(8,128)(2,1)} %refs_1_.1) | copy-start | bytes 4718596
  94.9 3.1 %copy-start.1 = (f32[24,2304]{1,0:T(8,128)S(1)}, f32[24,2304]{1,0:T(8,128)}, u32[]{:S(2)}) copy-start(f32[24,2304]{1,0:T(8,128)} %get-tuple-element.13) | copy-start | bytes 663556
  94.9 3.8 %copy-start.2 = (f32[24,768]{1,0:T(8,128)S(1)}, f32[24,768]{1,0:T(8,128)}, u32[]{:S(2)}) copy-start(f32[24,768]{1,0:T(8,128)} %get-tuple-element.14) | copy-start | bytes 221188

commit v3 on v2

--- a/solution.py
+++ b/solution.py
@@ -446,9 +446,10 @@
                 here = slice(16 * m, 16 * m + 16)
                 both = br[at_row, here].astype(F32)
                 lo, hi = both[:WIN], both[WIN:]
-                r["out"][at_row, here] = jnp.concatenate(
+                grad = jnp.concatenate(
                     [jnp.where(low, before, lo), jnp.where(low, lo, hi)], axis=0
-                ).astype(BF16)
+                )
+                r["out"][at_row, here] = (xg[1, at_row, here].astype(F32) + grad).astype(BF16)
                 before = hi
         return 0
 
@@ -488,6 +489,23 @@
         copy.wait_send()
     for ring in (*outer, *inner):
         ring.close()
+
+
+def hand_over(scene_in, qkv_in, proj_in, scene_grad, qkv_grad, proj_grad, a, b, c, come, go):
+    step = scene_in.shape[0] // 8
+    pieces = [(qkv_in, b, qkv_grad), (proj_in, c, proj_grad)]
+    for n in range(8):
+        here = pl.ds(n * step, step)
+        pieces.append((scene_in.at[here], a.at[here], scene_grad.at[here]))
+    loads = [pltpu.make_async_copy(x, y, come.at[n]) for n, (x, y, _) in enumerate(pieces)]
+    stores = [pltpu.make_async_copy(y, z, go.at[n]) for n, (_, y, z) in enumerate(pieces)]
+    for load in loads:
+        load.start()
+    for load, store in zip(loads, stores):
+        load.wait()
+        store.start()
+    for store in stores:
+        store.wait()
 
 
 def on_device(scene, cotangent, query_key_value_weight, proj_weight, kept):
@@ -546,7 +564,7 @@
     )
     anywhere = pl.BlockSpec(memory_space=pl.ANY)
     in_vmem = pl.BlockSpec(memory_space=pltpu.VMEM)
-    branch, qkv_grad, proj_grad = pl.pallas_call(
+    grads = pl.pallas_call(
         functools.partial(kernel, names),
         out_shape=(
             jax.ShapeDtypeStruct((rows, cols, width), BF16),
@@ -560,8 +578,14 @@
             collective_id=0, has_side_effects=True, vmem_limit_bytes=60 * 1024 * 1024
         ),
     )(scene, cotangent, query_key_value_weight, proj_weight, kept.T)
-    scene_grad = (cotangent.astype(F32) + branch.astype(F32)).astype(BF16)
-    return scene_grad, qkv_grad, proj_grad
+    return pl.pallas_call(
+        hand_over,
+        out_shape=tuple(jax.ShapeDtypeStruct(a.shape, a.dtype) for a in grads),
+        in_specs=[anywhere] * 3,
+        out_specs=(anywhere,) * 3,
+        scratch_shapes=[pltpu.VMEM(a.shape, a.dtype) for a in grads]
+        + [pltpu.SemaphoreType.DMA((10,)), pltpu.SemaphoreType.DMA((10,))],
+    )(*grads)
 
 
 def solution(mesh):

time: 100 us -> 98.6 us (0.986)
  other arithmetic: 3.06 us -> 0 us
  Pallas kernels: 94.3 us -> 97.3 us
  local copies, waits for them, and re-layouts: 1.33 us -> 0 us
    convert_element_type x1 -> x0, other arithmetic: 3.06 us -> none  [on_device(): scene_grad = (cotangent.astype(F32) + branch.astype(F32)).astype(BF16)]
    pallas_call x0 -> x1, Pallas kernels: none -> 2.44 us  [on_device(): pl.pallas_call(hand_over, out_shape=tuple((jax.ShapeDtypeStruct(a.shape,...]
    unnamed x8 -> x0, local copies, waits for them, and re-layouts: 1.33 us -> none
where the time goes in v3:
time: 98.6 us; the launch traced here: 98 us
  Pallas kernels  97.3 us (99%)
    pallas_call x1, Pallas kernels, on_device(): pl.pallas_call(functools.partial(kernel, names), out_shape=(jax.ShapeDtyp...  94.9 us
    pallas_call x1, Pallas kernels, on_device(): pl.pallas_call(hand_over, out_shape=tuple((jax.ShapeDtypeStruct(a.shape,...  2.44 us

profile of v3, /device:TPU:32, one launch (start us, length us, event | category | flops | bytes accessed | tf_op | source)
XLA Modules:
  0.0 98.0 jit_solution(7785019412270071434)
XLA Ops:
  0.6 94.9 %shard_map.76 = (bf16[16,64,768]{2,1,0:T(8,128)(2,1)}, f32[24,2304]{1,0:T(8,128)}, f32[24,768]{1,0:T(8,128)}) custom-call(bf16[16,64,768]{2,1,0:T(8,128)(2,1)} %refs_0_.1, bf16[16,64,768]{2,1,0:T(8,128)(2,1)} %refs_1_.1, bf16[768,2304]{1,0:T(8,128)(2,1)} %refs_2_.1, bf16[768,768]{1,0:T(8,128)(2,1)} %refs_3_.1, s32[16,32]{1,0:T(8,128)} %bitcast.1), custom_call_target="tpu_custom_call" | custom-call | tf_op jit(solution)/shard_map/pallas_call | solution.py:567
  95.5 2.4 %shard_map.77 = (bf16[16,64,768]{2,1,0:T(8,128)(2,1)}, f32[24,2304]{1,0:T(8,128)}, f32[24,768]{1,0:T(8,128)}) custom-call(bf16[16,64,768]{2,1,0:T(8,128)(2,1)} %get-tuple-element.6.scene_in, f32[24,2304]{1,0:T(8,128)} %get-tuple-element.7.qkv_in, f32[24,768]{1,0:T(8,128)} %get-tuple-element.8.proj_in), custom_call_target="tpu_custom_call" | custom-call | tf_op jit(solution)/shard_map/pallas_call | solution.py:581

commit v4 on v3

--- a/solution.py
+++ b/solution.py
@@ -176,9 +176,50 @@
             grads[q, here] = dot(lhs, rhs)
         return 0
 
+    def place_of(p):
+        i = p // pairs
+        return i, p + i * (2 * pairs - 1 - 2 * p)
+
+    def finish(p):
+        i, m = place_of(p)
+        first = pl.multiple_of(p * BATCH, BATCH)
+        here = pl.ds(pl.multiple_of(16 * m, 16), 16)
+        r["dxh"][...] = dot(stash_d[pl.ds(first, BATCH)], wqkv_t[...])
+
+        last = []
+        for at_row in range(WIN):
+            tiles = []
+            for w in (0, 1):
+                near_row = slice(w * AREA + WIN * at_row, w * AREA + WIN * (at_row + 1))
+                grad, normed = r["dxh"][near_row], xh_s[near_row]
+                inverse = inv_s[near_row][:, :1]
+                tiles.append(
+                    inverse
+                    * (
+                        grad
+                        - jnp.mean(grad, axis=-1, keepdims=True)
+                        - normed * jnp.mean(grad * normed, axis=-1, keepdims=True)
+                    )
+                )
+            br[HALF + WIN * i + at_row, here] = jnp.concatenate(tiles, axis=0).astype(BF16)
+            r["last"][at_row] = tiles[1]
+
+        @pl.when(m == pairs - 1)
+        def _():
+            last = r["last"][...]
+            packed = [
+                jnp.where(low, last[2 * n], swap_halves(last[2 * n + 1])) for n in range(WIN // 2)
+            ]
+            edge_ret[pl.ds(pl.multiple_of(32 * i, 32), 32)] = jnp.concatenate(
+                packed, axis=0
+            ).astype(BF16)
+
     def step(p, _):
-        i = p // pairs
-        m = p + i * (2 * pairs - 1 - 2 * p)
+        i, m = place_of(p)
+
+        @pl.when(p > 0)
+        def _():
+            finish(p - 1)
 
         @pl.when(p == 2)
         def _():
@@ -292,41 +333,9 @@
             stash_d[far[w], part(2, g)] = d_v[n].astype(BF16)
 
         stash_at[:, pl.ds(first, BATCH)] = att_s[...].T
-        r["dxh"][...] = dot(stash_d[pl.ds(first, BATCH)], wqkv_t[...])
-
-        last = []
-        for at_row in range(WIN):
-            tiles = []
-            for w in (0, 1):
-                near_row = slice(w * AREA + WIN * at_row, w * AREA + WIN * (at_row + 1))
-                grad, normed = r["dxh"][near_row], xh_s[near_row]
-                inverse = inv_s[near_row][:, :1]
-                tiles.append(
-                    inverse
-                    * (
-                        grad
-                        - jnp.mean(grad, axis=-1, keepdims=True)
-                        - normed * jnp.mean(grad * normed, axis=-1, keepdims=True)
-                    )
-                )
-            br[HALF + WIN * i + at_row, here] = jnp.concatenate(tiles, axis=0).astype(BF16)
-            r["last"][at_row] = tiles[1]
-
-        @pl.when(m == pairs - 1)
-        def _():
-            last = r["last"][...]
-            packed = [
-                jnp.where(low, last[2 * n], swap_halves(last[2 * n + 1])) for n in range(WIN // 2)
-            ]
-            edge_ret[pl.ds(pl.multiple_of(32 * i, 32), 32)] = jnp.concatenate(
-                packed, axis=0
-            ).astype(BF16)
-
         return 0
 
     lax.fori_loop(0, 2 * pairs, step, 0)
-    corner_down.start()
-    row_back.start()
 
     share = width // (nrow * ncol)
     parts = [r["part_%d" % q] for q in range(4)]
@@ -449,7 +458,7 @@
                 grad = jnp.concatenate(
                     [jnp.where(low, before, lo), jnp.where(low, lo, hi)], axis=0
                 )
-                r["out"][at_row, here] = (xg[1, at_row, here].astype(F32) + grad).astype(BF16)
+                r["out_v"][at_row, here] = (xg[1, at_row, here].astype(F32) + grad).astype(BF16)
                 before = hi
         return 0
 
@@ -458,10 +467,18 @@
         close_grads(q)
         outer[q].begin()
         outer[q].go_on()
+    finish(jnp.int32(2 * pairs - 1))
+    corner_down.start()
+    row_back.start()
     for q in order:
         outer[q].pass_on()
     col_back.wait_recv()
     lax.fori_loop(1, tile_rows // 4, place, 0)
+    stores = [
+        pltpu.make_async_copy(r["out_v"].at[rows], r["out"].at[rows], r["load_sems"].at[4 + n])
+        for n, rows in enumerate((pl.ds(HALF, tile_rows - HALF), pl.ds(0, HALF)))
+    ]
+    stores[0].start()
     for q in order:
         turn(q)
     corner_down.wait_recv()
@@ -471,6 +488,7 @@
     row_back.wait_recv()
     corner_right.wait_recv()
     lax.fori_loop(0, 1, place, 0)
+    stores[1].start()
     for q in order:
         cross(q)
     for q in (0, 2, 1, 3):
@@ -489,6 +507,8 @@
         copy.wait_send()
     for ring in (*outer, *inner):
         ring.close()
+    for store in stores:
+        store.wait()
 
 
 def hand_over(scene_in, qkv_in, proj_in, scene_grad, qkv_grad, proj_grad, a, b, c, come, go):
@@ -522,6 +542,7 @@
         "stash_xt": ((width, all_tokens), BF16),
         "stash_at": ((width, all_tokens), BF16),
         "grads": ((4, width, width), F32),
+        "out_v": ((rows, cols, width), BF16),
         "xb": ((BATCH, width), BF16),
         "xh": ((BATCH, width), F32),
         "inv": ((BATCH, 128), F32),
@@ -553,7 +574,7 @@
         vmem["relay_next_%d" % q] = ((2, *piece), BF16)
         vmem["direct_next_%d" % q] = ((2, 2, *piece), BF16)
     sems = {
-        "load_sems": pltpu.SemaphoreType.DMA((4,)),
+        "load_sems": pltpu.SemaphoreType.DMA((6,)),
         "send_sems": pltpu.SemaphoreType.DMA((68,)),
         "recv_sems": pltpu.SemaphoreType.DMA((68,)),
     }
@@ -572,7 +593,7 @@
             jax.ShapeDtypeStruct((share, width), F32),
         ),
         in_specs=[anywhere] * 4 + [pl.BlockSpec(memory_space=pltpu.SMEM)],
-        out_specs=(in_vmem,) * 3,
+        out_specs=(anywhere, in_vmem, in_vmem),
         scratch_shapes=[pltpu.VMEM(*spec) for spec in vmem.values()] + list(sems.values()),
         compiler_params=pltpu.CompilerParams(
             collective_id=0, has_side_effects=True, vmem_limit_bytes=60 * 1024 * 1024

time: 98.6 us -> 97.3 us (0.987)
  Pallas kernels: 97.3 us -> 96.2 us
    pallas_call x1, Pallas kernels: 94.9 us -> 93.7 us  [on_device(): pl.pallas_call(functools.partial(kernel, names), out_shape=(jax.ShapeDtyp...]
where the time goes in v4:
time: 97.3 us; the launch traced here: 96.8 us
  Pallas kernels  96.2 us (99%)
    pallas_call x1, Pallas kernels, on_device(): pl.pallas_call(functools.partial(kernel, names), out_shape=(jax.ShapeDtyp...  93.7 us
    pallas_call x1, Pallas kernels, on_device(): pl.pallas_call(hand_over, out_shape=tuple((jax.ShapeDtypeStruct(a.shape,...  2.44 us

profile of v4, /device:TPU:32, one launch (start us, length us, event | category | flops | bytes accessed | tf_op | source)
XLA Modules:
  0.0 96.8 jit_solution(13570730969758259823)
XLA Ops:
  0.6 93.7 %shard_map.76 = (bf16[16,64,768]{2,1,0:T(8,128)(2,1)}, f32[24,2304]{1,0:T(8,128)}, f32[24,768]{1,0:T(8,128)}) custom-call(bf16[16,64,768]{2,1,0:T(8,128)(2,1)} %refs_0_.1, bf16[16,64,768]{2,1,0:T(8,128)(2,1)} %refs_1_.1, bf16[768,2304]{1,0:T(8,128)(2,1)} %refs_2_.1, bf16[768,768]{1,0:T(8,128)(2,1)} %refs_3_.1, s32[16,32]{1,0:T(8,128)} %bitcast.1), custom_call_target="tpu_custom_call" | custom-call | tf_op jit(solution)/shard_map/pallas_call | solution.py:588
  94.4 2.4 %shard_map.77 = (bf16[16,64,768]{2,1,0:T(8,128)(2,1)}, f32[24,2304]{1,0:T(8,128)}, f32[24,768]{1,0:T(8,128)}) custom-call(bf16[16,64,768]{2,1,0:T(8,128)(2,1)} %get-tuple-element.6.scene_in, f32[24,2304]{1,0:T(8,128)} %get-tuple-element.7.qkv_in, f32[24,768]{1,0:T(8,128)} %get-tuple-element.8.proj_in), custom_call_target="tpu_custom_call" | custom-call | tf_op jit(solution)/shard_map/pallas_call | solution.py:602

commit v5 on v4

--- a/solution.py
+++ b/solution.py
@@ -358,7 +358,12 @@
                         parts[q][y, z, x] = piece
             return 0
 
-        lax.fori_loop(0, 4, body, 0, unroll=4)
+        for n in range(4):
+            body((x_at + 2 + n) % 4 if q < 2 else n, 0)
+            if q < 2 and n == 0:
+                outer[q].begin()
+        if q >= 2:
+            outer[q].begin()
 
     class Ring:
         def __init__(self, base, part, me, forward, backward, relay, direct):
@@ -465,7 +470,6 @@
     order = (0, 2, 1, 3)
     for q in order:
         close_grads(q)
-        outer[q].begin()
         outer[q].go_on()
     finish(jnp.int32(2 * pairs - 1))
     corner_down.start()
@@ -513,10 +517,11 @@
 
 def hand_over(scene_in, qkv_in, proj_in, scene_grad, qkv_grad, proj_grad, a, b, c, come, go):
     step = scene_in.shape[0] // 8
-    pieces = [(qkv_in, b, qkv_grad), (proj_in, c, proj_grad)]
+    pieces = []
     for n in range(8):
         here = pl.ds(n * step, step)
         pieces.append((scene_in.at[here], a.at[here], scene_grad.at[here]))
+    pieces += [(qkv_in, b, qkv_grad), (proj_in, c, proj_grad)]
     loads = [pltpu.make_async_copy(x, y, come.at[n]) for n, (x, y, _) in enumerate(pieces)]
     stores = [pltpu.make_async_copy(y, z, go.at[n]) for n, (_, y, z) in enumerate(pieces)]
     for load in loads:

time: 97.3 us -> 96.8 us (level)
  no operation moved by 1% of the time
where the time goes in v5:
time: 96.8 us; the launch traced here: 96.5 us
  Pallas kernels  95.8 us (99%)
    pallas_call x1, Pallas kernels, on_device(): pl.pallas_call(functools.partial(kernel, names), out_shape=(jax.ShapeDtyp...  93.4 us
    pallas_call x1, Pallas kernels, on_device(): pl.pallas_call(hand_over, out_shape=tuple((jax.ShapeDtypeStruct(a.shape,...  2.42 us

profile of v5, /device:TPU:32, one launch (start us, length us, event | category | flops | bytes accessed | tf_op | source)
XLA Modules:
  0.0 96.5 jit_solution(6965636259512657828)
XLA Ops:
  0.6 93.4 %shard_map.76 = (bf16[16,64,768]{2,1,0:T(8,128)(2,1)}, f32[24,2304]{1,0:T(8,128)}, f32[24,768]{1,0:T(8,128)}) custom-call(bf16[16,64,768]{2,1,0:T(8,128)(2,1)} %refs_0_.1, bf16[16,64,768]{2,1,0:T(8,128)(2,1)} %refs_1_.1, bf16[768,2304]{1,0:T(8,128)(2,1)} %refs_2_.1, bf16[768,768]{1,0:T(8,128)(2,1)} %refs_3_.1, s32[16,32]{1,0:T(8,128)} %bitcast.1), custom_call_target="tpu_custom_call" | custom-call | tf_op jit(solution)/shard_map/pallas_call | solution.py:593
  94.1 2.4 %shard_map.77 = (bf16[16,64,768]{2,1,0:T(8,128)(2,1)}, f32[24,2304]{1,0:T(8,128)}, f32[24,768]{1,0:T(8,128)}) custom-call(bf16[16,64,768]{2,1,0:T(8,128)(2,1)} %get-tuple-element.6.scene_in, f32[24,2304]{1,0:T(8,128)} %get-tuple-element.7.qkv_in, f32[24,768]{1,0:T(8,128)} %get-tuple-element.8.proj_in), custom_call_target="tpu_custom_call" | custom-call | tf_op jit(solution)/shard_map/pallas_call | solution.py:607
